TPU v7x, 256 devices: a whole 4x4x8 slice. The times are simulated.
256 devices in a mesh: dp: 8 (over x, z_hi), tensor: 32 (over y, z_lo, core).
Axes of the slice: x: 4, y: 4, z: 8 (z_hi: 2, z_lo: 4; z = z_hi * 4 + z_lo), core: 2. Of those that a mesh axis runs over, the one named last changes fastest.
Arguments:
- block_input: bfloat16 [3072, 6144], P('dp', 'tensor'), may hold values from -6 to 6
- output_gradient: bfloat16 [3072, 6144], P('dp', 'tensor'), may hold values from -6 to 6
- attn_grad: bfloat16 [3072, 6144], P('dp', 'tensor'), may hold values from -6 to 6
- layernorm_gain: float32 [6144], replicated, may hold values from 0.5 to 1.5
- w_in: bfloat16 [6144, 12288], P(None, 'tensor'), may hold values from -0.078125 to 0.078125
- w_out: bfloat16 [12288, 6144], P('tensor'), may hold values from -0.0546875 to 0.0546875
Outputs:
- input_gradient: bfloat16 [3072, 6144], P('dp', 'tensor')
- gain_gradient: float32 [6144], P('tensor')
- w_in_grad: float32 [6144, 12288], P('dp', 'tensor')
- w_out_grad: float32 [12288, 6144], P('tensor', 'dp')
All inputs are finite; a program needn't handle non-finite values.
Results may differ from a plain program's by a relative error of at most 0.018.
Values may be sent and summed in bfloat16 or wider, within the bound.
A program may use at most 128 MiB of HBM per device.

v0:
```python
import math

import jax
import jax.numpy as jnp
from jax import lax
from jax.sharding import PartitionSpec as P

gelu_coef = math.sqrt(2.0 / math.pi)


def gelu_value(value):
    inner = gelu_coef * (value + 0.044715 * value * value * value)
    return 0.5 * value * (1.0 + jnp.tanh(inner))


def gelu_slope(value):
    inner = gelu_coef * (value + 0.044715 * value * value * value)
    tanh_val = jnp.tanh(inner)
    return 0.5 * (1.0 + tanh_val) + 0.5 * value * (1.0 - tanh_val * tanh_val) * gelu_coef * (
        1.0 + 3.0 * 0.044715 * value * value
    )


def on_device(block_input, output_gradient, attn_grad, layernorm_gain, w_in, w_out):
    portion_width = block_input.shape[1]
    gathered_x, gathered_grad = (
        lax.all_gather(block_input, "tensor", axis=1, tiled=True),
        lax.all_gather(output_gradient, "tensor", axis=1, tiled=True),
    )
    full_width = gathered_x.shape[1]
    worker_position = lax.axis_index("tensor")
    gain_own = lax.dynamic_slice_in_dim(
        layernorm_gain, worker_position * portion_width, portion_width, 0
    )
    values = gathered_x.astype(jnp.float32)
    row_mean = jnp.mean(values, axis=1, keepdims=True)
    centered_input = values - row_mean
    variance = jnp.mean(centered_input * centered_input, axis=1, keepdims=True)
    inverse_deviation = lax.rsqrt(variance + 1e-06)
    standardized_input = centered_input * inverse_deviation
    normalized_input = (standardized_input * layernorm_gain).astype(jnp.bfloat16)
    pre_act = jnp.dot(normalized_input, w_in, preferred_element_type=jnp.float32)
    hidden_act = gelu_value(pre_act).astype(jnp.bfloat16)
    act_grad = jnp.dot(gathered_grad, w_out.T, preferred_element_type=jnp.float32)
    hidden_grad = (act_grad * gelu_slope(pre_act)).astype(jnp.bfloat16)
    partial_value = jnp.dot(hidden_grad, w_in.T, preferred_element_type=jnp.float32)
    standardized_local = lax.dynamic_slice_in_dim(
        standardized_input, worker_position * portion_width, portion_width, 1
    )
    attn_vals = attn_grad.astype(jnp.float32)
    reduced = lax.psum_scatter(
        partial_value.astype(jnp.bfloat16), "tensor", scatter_dimension=1, tiled=True
    ).astype(jnp.float32)
    normalized_gradient = reduced + attn_vals
    scaled_gradient = normalized_gradient * gain_own
    first_sum, second_sum = lax.psum(
        (jnp.sum(scaled_gradient, axis=1), jnp.sum(scaled_gradient * standardized_local, axis=1)),
        "tensor",
    )
    first_moment = (first_sum / full_width)[:, None]
    second_moment = (second_sum / full_width)[:, None]
    input_gradient = (
        output_gradient.astype(jnp.float32)
        + (scaled_gradient - first_moment - standardized_local * second_moment) * inverse_deviation
    ).astype(jnp.bfloat16)
    gain_gradient = lax.psum(jnp.sum(normalized_gradient * standardized_local, axis=0), "dp")
    w_in_grad = lax.psum_scatter(
        jnp.dot(normalized_input.T, hidden_grad, preferred_element_type=jnp.float32).astype(
            jnp.bfloat16
        ),
        "dp",
        scatter_dimension=0,
        tiled=True,
    ).astype(jnp.float32)
    out_term = jnp.dot(hidden_act.T, gathered_grad, preferred_element_type=jnp.float32)
    w_out_grad = lax.psum_scatter(
        out_term.astype(jnp.bfloat16), "dp", scatter_dimension=1, tiled=True
    ).astype(jnp.float32)
    return (input_gradient, gain_gradient, w_in_grad, w_out_grad)


def solution(mesh):
    placed = (
        P("dp", "tensor"),
        P("dp", "tensor"),
        P("dp", "tensor"),
        P(),
        P(None, "tensor"),
        P("tensor", None),
    )
    return jax.shard_map(
        on_device,
        mesh=mesh,
        in_specs=placed,
        out_specs=(P("dp", "tensor"), P("tensor"), P("dp", "tensor"), P("tensor", "dp")),
        check_vma=False,
    )
```

profile of v0, /device:TPU:97, one launch (start us, length us, event | category | flops | bytes accessed | tf_op | source)
XLA Modules:
  0.0 580.8 jit_solution(7574647677203751378)
XLA Ops:
  7.2 0.7 all-gather.5.cloned.1.call-update
  8.0 0.7 all-gather.3.cloned.1.call-update
  8.7 65.9 %all-gather.5.cloned.1.call-done = bf16[384,6144]{0,1:T(8,128)(2,1)} async-done(((bf16[384,192]{0,1:T(8,128)(2,1)}), bf16[384,6144]{0,1:T(8,128)(2,1)}) %all-gather.5.cloned.1.call-update) | async-done | bytes 4718608 | tf_op jit(solution)/shard_map/all_gather | solution.py:27
  74.6 3.3 convert_reduce_fusion
  77.9 0.4 copy-done
  78.3 1.3 fusion.2
  79.6 0.1 copy-done.1
  79.7 3.8 fusion.4
  83.5 55.7 %all-gather.3.cloned.1.call-done = bf16[384,6144]{0,1:T(8,128)(2,1)} async-done(((bf16[384,192]{0,1:T(8,128)(2,1)}), bf16[384,6144]{0,1:T(8,128)(2,1)}) %all-gather.3.cloned.1.call-update) | async-done | bytes 4718608 | tf_op jit(solution)/shard_map/all_gather | solution.py:28
  139.2 7.2 %convolution_convert_fusion = bf16[384,6144]{1,0:T(8,128)(2,1)} fusion(bf16[384,6144]{0,1:T(8,128)(2,1)} %all-gather.3.cloned.1.call-done, f32[384,384]{1,0:T(8,128)S(1)} %fusion.4), kind=kOutput, calls=%fused_computation.6 | convolution fusion | flops 1815625728 | bytes 10027008 | tf_op jit(solution)/shard_map/dot_general | solution.py:75
  146.4 0.2 reduce-scatter.4.cloned.1.call-start
  146.6 6.6 %fusion.3 = bf16[384,384]{1,0:T(8,128)(2,1)S(1)} fusion(bf16[384,6144]{0,1:T(8,128)(2,1)} %all-gather.3.cloned.1.call-done, bf16[384,6144]{1,0:T(8,128)(2,1)} %param.11, f32[384,384]{1,0:T(8,128)S(1)} %fusion.4), kind=kOutput, calls=%fused_computation.10 | convolution fusion | flops 1814740992 | bytes 10321920 | tf_op jit(solution)/shard_map/dot_general | solution.py:44
  153.2 7.5 %convolution_convert_fusion.2 = bf16[384,6144]{0,1:T(8,128)(2,1)} fusion(bf16[384,384]{1,0:T(8,128)(2,1)S(1)} %fusion.3, bf16[6144,384]{1,0:T(8,128)(2,1)} %param.10), kind=kOutput, calls=%fused_computation.8 | convolution fusion | flops 1814298624 | bytes 9732096 | tf_op jit(solution)/shard_map/dot_general | solution.py:46
  160.8 6.6 %convolution_convert_fusion.1 = bf16[6144,384]{1,0:T(8,128)(2,1)} fusion(bf16[384,384]{1,0:T(8,128)(2,1)S(1)} %fusion.3, f32[6144]{0:T(1024)S(1)} %copy-done.4, f32[384]{0:T(512)S(1)} %add_rsqrt_fusion, f32[384]{0:T(512)S(1)} %broadcast_multiply_fusion.2, bf16[384,6144]{0,1:T(8,128)(2,1)} %all-gather.5.cloned.1.call-done), kind=kOutput, calls=%fused_computation.7 | convolution fusion | flops 1826095104 | bytes 9759744 | tf_op jit(solution)/shard_map/dot_general | solution.py:68
  167.6 6.9 %fusion = f32[384,6144]{0,1:T(8,128)} fusion(bf16[384,6144]{0,1:T(8,128)(2,1)} %all-gather.5.cloned.1.call-done, f32[384]{0:T(512)S(1)} %add_rsqrt_fusion, f32[384]{0:T(512)S(1)} %broadcast_multiply_fusion.2), kind=kLoop, calls=%fused_computation.2 | loop fusion | flops 7077888 | bytes 14158848 | tf_op jit(solution)/shard_map/mul | solution.py:40
  174.5 103.3 %reduce-scatter.8.cloned.1.call-done = bf16[384,768]{1,0:T(8,128)(2,1)} async-done(((bf16[384,6144]{1,0:T(8,128)(2,1)}), bf16[384,768]{1,0:T(8,128)(2,1)}) %reduce-scatter.8.cloned.1.call-update) | async-done | bytes 589840 | tf_op jit(solution)/shard_map/reduce_scatter | solution.py:76
  277.8 2.2 convert_element_type.51
  280.0 132.9 %reduce-scatter.4.cloned.1.call-done = bf16[384,192]{0,1:T(8,128)(2,1)} async-done(((bf16[384,6144]{0,1:T(8,128)(2,1)}), bf16[384,192]{0,1:T(8,128)(2,1)}) %reduce-scatter.4.cloned.1.call-update) | async-done | bytes 147472 | tf_op jit(solution)/shard_map/reduce_scatter | solution.py:51
  412.9 1.2 multiply_reduce_fusion
  414.1 27.4 %psum.23 = f32[192]{0:T(256)} all-reduce(f32[192]{0:T(256)S(1)} %get-tuple-element.4), channel_id=1, replica_groups=mesh['dp'=8,'tensor'=32] {'dp'}, use_global_device_ids=true, to_apply=%region_8.0 | all-reduce | flops 192 | bytes 1536 | tf_op jit(solution)/shard_map/psum | solution.py:66
  441.5 83.5 %all-reduce = (f32[384]{0:T(512)S(1)}, f32[384]{0:T(512)S(1)}) all-reduce(f32[384]{0:T(512)S(1)} %get-tuple-element.5, f32[384]{0:T(512)S(1)} %get-tuple-element.6), channel_id=1, replica_groups=mesh['dp'=8,'tensor'=32] {'tensor'}, use_global_device_ids=true, to_apply=%region_6.0 | all-reduce | flops 768 | bytes 6144 | tf_op jit(solution)/shard_map/psum | solution.py:56
  525.0 45.2 %reduce-scatter.6.cloned.1.call-done = bf16[768,384]{1,0:T(8,128)(2,1)} async-done(((bf16[6144,384]{1,0:T(8,128)(2,1)}), bf16[768,384]{1,0:T(8,128)(2,1)}) %reduce-scatter.6.cloned.1.call-update) | async-done | bytes 589840 | tf_op jit(solution)/shard_map/reduce_scatter | solution.py:67
  570.3 2.2 convert_element_type.48
  572.4 1.8 add_convert_fusion
  (19 shorter events, 0.3 us)
Async XLA Ops:
  7.2 67.4 %all-gather.5.cloned.1.call-start = ((), (), s32[]{:S(2)}) async-start(), calls=%async_computation.4 | async-start | bytes 4866048 | tf_op jit(solution)/shard_map/all_gather | solution.py:27
  7.9 131.3 %all-gather.3.cloned.1.call-start = ((), (), s32[]{:S(2)}) async-start(), calls=%async_computation.3 | async-start | bytes 4866048 | tf_op jit(solution)/shard_map/all_gather | solution.py:28
  7.9 71.7 %copy-start.4 = (f32[6144]{0:T(1024)S(1)}, f32[6144]{0:T(1024)}, u32[]{:S(2)}) copy-start(f32[6144]{0:T(1024)} %param.9) | copy-start | bytes 73732
  8.6 269.2 %reduce-scatter.8.cloned.1.call-start = ((), (), s32[]{:S(2)}) async-start(), calls=%async_computation.7 | async-start | bytes 5308416 | tf_op jit(solution)/shard_map/reduce_scatter | solution.py:76
  74.5 3.8 copy-start
  74.5 5.2 copy-start.1
  146.4 266.5 %reduce-scatter.4.cloned.1.call-start = ((), (), s32[]{:S(2)}) async-start(), calls=%async_computation.5 | async-start | bytes 4866048 | tf_op jit(solution)/shard_map/reduce_scatter | solution.py:51
  160.8 409.5 %reduce-scatter.6.cloned.1.call-start = ((), (), s32[]{:S(2)}) async-start(), calls=%async_computation.6 | async-start | bytes 5308416 | tf_op jit(solution)/shard_map/reduce_scatter | solution.py:67
  167.6 245.3 %copy-start.3 = (bf16[384,192]{0,1:T(8,128)(2,1)S(1)}, bf16[384,192]{0,1:T(8,128)(2,1)}, u32[]{:S(2)}) copy-start(bf16[384,192]{0,1:T(8,128)(2,1)} %param.8) | copy-start | bytes 442372
  167.6 404.9 %copy-start.2 = (bf16[384,192]{0,1:T(8,128)(2,1)S(1)}, bf16[384,192]{0,1:T(8,128)(2,1)}, u32[]{:S(2)}) copy-start(bf16[384,192]{0,1:T(8,128)(2,1)} %param.7) | copy-start | bytes 442372
Sparse Core Ops, SparseCore 0:
  9.9 64.6 all-gather.4
  76.4 62.7 all-gather.2
  146.5 131.2 reduce-scatter.7
  280.4 132.4 reduce-scatter.3
  417.6 152.6 reduce-scatter.5
where the time goes:
time: 586 us; the launch traced here: 581 us
  waiting for transfers between devices  404 us (69%)
  blocking collectives  111 us (19%)
  matrix products  31.7 us (5%)
  other arithmetic  18.9 us (3%)
  between operations  13.8 us (2%)
    reduce_scatter x1, waiting for transfers between devices, on_device(): lax.psum_scatter(partial_value.astype(jnp.bfloat16), 'tensor', scatter_di...  133 us
    reduce_scatter x1, waiting for transfers between devices, on_device(): lax.psum_scatter(out_term.astype(jnp.bfloat16), 'dp', scatter_dimension=1...  103 us
    psum x1, blocking collectives, on_device(): lax.psum((jnp.sum(scaled_gradient, axis=1), jnp.sum(scaled_gradient * sta...  83.5 us
    all_gather x1, waiting for transfers between devices, on_device(): lax.all_gather(block_input, 'tensor', axis=1, tiled=True)  65.9 us
    all_gather x1, waiting for transfers between devices, on_device(): lax.all_gather(output_gradient, 'tensor', axis=1, tiled=True)  55.7 us
    reduce_scatter x1, waiting for transfers between devices, on_device(): lax.psum_scatter(jnp.dot(normalized_input.T, hidden_grad, preferred_eleme...  45.2 us
    psum x1, blocking collectives, on_device(): lax.psum(jnp.sum(normalized_gradient * standardized_local, axis=0), 'dp')  27.4 us
  transfers between devices with their start and end apart: 5, of which 5 were waited for; matrix products, arithmetic and copies ran while one was open for 7% of the time, Pallas kernels for 0%

commit v1 on v0

v1 whole, which is shorter than its diff:
```python
import functools
import math

import jax
import jax.numpy as jnp
from jax import lax
from jax.experimental import pallas as pl
from jax.experimental.pallas import tpu as pltpu
from jax.sharding import PartitionSpec as P

MESH = pl.DeviceIdType.MESH
F32, BF16 = jnp.float32, jnp.bfloat16
COEF = math.sqrt(2.0 / math.pi)
TOK = 384
HID = 384
ROWS = 192
CHIP = 384
D = 6144

NT = (((1,), (1,)), ((), ()))


def dot(a, b):
    return jnp.dot(a, b, preferred_element_type=F32)


def dot_nt(a, b):
    return lax.dot_general(a, b, NT, preferred_element_type=F32)


def wide(column):
    return jnp.concatenate([column] * (TOK // 128), axis=1)


def kernel(
    x_in, g_in, attn, gain, w_in, w_out,
    dx_out, gg_out, dwin_out, dwout_out,
    XG, XS, XN, WI, WT, WO, HB, GB, PRE, ACT, SM, SV, ST, R1, R2, R3, R4, TS, MO, GP,
    zs, zr, as_, ar, z2s, z2r, a2s, a2r, ps, pr, hs, hr, z4s, z4r, xs, xr, xbs, xbr,
    r1s, r1r, r2s, r2r, r3s, r3r, r4s, r4r, sts, str_, mos, mor, gps, gpr, loc,
):
    dp, tensor = lax.axis_index("dp"), lax.axis_index("tensor")
    x, h = dp // 2, dp % 2
    y, l, c = tensor // 8, (tensor // 2) % 4, tensor % 2
    chip = y * 4 + l

    def dev(x_, h_, y_, l_, c_):
        return (x_ * 2 + h_, y_ * 8 + l_ * 2 + c_)

    def mod4(v):
        return lax.rem(v, 4)

    sib = dev(x, h, y, l, 1 - c)
    yat = [dev(x, h, mod4(y + o), l, c) for o in range(4)]
    zat = [dev(x, h, y, mod4(l + o), c) for o in range(4)]
    xat = [dev(mod4(x + o), h, y, l, c) for o in range(4)]
    opposite = dev(x, 1 - h, y, l, c)
    dpat = [(lax.rem(dp + o, 8), tensor) for o in range(8)]
    crossing = lax.rem(l // 2 + h, 2)

    sends = []

    def copy(src, dst, send, recv, to):
        return pltpu.make_async_remote_copy(
            src_ref=src, dst_ref=dst, send_sem=send, recv_sem=recv, device_id=to, device_id_type=MESH
        )

    def put(src, dst, send, recv, to):
        made = copy(src, dst, send, recv, to)
        made.start()
        sends.append(made)

    def got(dst, recv):
        copy(dst, dst, recv, recv, sib).wait_recv()

    barrier = pltpu.get_barrier_semaphore()
    for to in [sib] + yat[1:] + zat[1:] + dpat[1:] + [dev(y, 1 - h, x, 2 * h + lax.rem(l, 2), c)]:
        pl.semaphore_signal(barrier, inc=1, device_id=to, device_id_type=MESH)

    own_x = pltpu.make_async_copy(x_in, XG.at[0, chip, c], loc.at[0])
    own_g = pltpu.make_async_copy(g_in, XG.at[1, chip, c], loc.at[1])
    load_wi = pltpu.make_async_copy(w_in, WI, loc.at[2])
    own_x.start()
    own_g.start()
    load_wi.start()

    def load_wo(j):
        return pltpu.make_async_copy(w_out.at[:, pl.ds(j * CHIP, CHIP)], WO.at[j], loc.at[3 + j])

    for j in range(16):
        load_wo(j).start()
    own_x.wait()
    own_g.wait()
    pl.semaphore_wait(barrier, 14 + 2 * crossing)

    def ring(n, ready, view, half, plus, minus, ss, rs, other=None):
        def first(i):
            ready(i)
            put(view(i, 0), view(i, 0), ss.at[i, 0], rs.at[i, 1], plus)
            put(view(i, 0), view(i, 0), ss.at[i, 1], rs.at[i, 0], minus)
            if other:
                put(view(i, 0), view(i, 0), ss.at[i, 4], rs.at[i, 4], sib)

        def second(i):
            got(view(i, 1), rs.at[i, 0])
            put(half(i, 1, 1), half(i, 1, 1), ss.at[i, 3], rs.at[i, 3], minus)
            got(view(i, 3), rs.at[i, 1])
            put(half(i, 3, 0), half(i, 3, 0), ss.at[i, 2], rs.at[i, 2], plus)
            if other:
                put(view(i, 1), view(i, 1), ss.at[i, 5], rs.at[i, 5], sib)
                put(view(i, 3), view(i, 3), ss.at[i, 7], rs.at[i, 7], sib)

        def third(i):
            got(half(i, 2, 0), rs.at[i, 2])
            got(half(i, 2, 1), rs.at[i, 3])
            if other:
                put(view(i, 2), view(i, 2), ss.at[i, 6], rs.at[i, 6], sib)

        def last(i):
            if other:
                for o in (0, 1, 3, 2):
                    got(other(i, o), rs.at[i, 4 + o])

        for t in range(n + 3):
            if t < n:
                first(t)
            if 0 <= t - 1 < n:
                second(t - 1)
            if 0 <= t - 2 < n:
                third(t - 2)
            if 0 <= t - 3 < n:
                last(t - 3)
                yield t - 3
            else:
                yield None

    def chip_at(i, o):
        return mod4(y + o) * 4 + mod4(l + i)

    def gather(a):
        def ready(i):
            if i > 0:
                got(XG.at[a, chip_at(i, 0), c], zr.at[a, i])

        return ring(
            4, ready,
            lambda i, o: XG.at[a, chip_at(i, o), c],
            lambda i, o, q: XG.at[a, chip_at(i, o), c, q],
            yat[1], yat[3], as_.at[a], ar.at[a],
            lambda i, o: XG.at[a, chip_at(i, o), 1 - c],
        )

    def slice_at(i, o, c_):
        lp = mod4(l + i)
        return (lp // 2, 2 * (2 * mod4(y + o) + (1 - h)) + lax.rem(lp, 2), c_)

    def slices():
        def ready(i):
            if i > 0:
                got(XS.at[slice_at(i, 0, c)], z2r.at[i])

        return ring(
            4, ready,
            lambda i, o: XS.at[slice_at(i, o, c)],
            lambda i, o, q: XS.at[slice_at(i, o, c) + (q,)],
            yat[1], yat[3], a2s, a2r,
            lambda i, o: XS.at[slice_at(i, o, 1 - c)],
        )

    def hidden_ring(a):
        def at(i, o):
            return (a, 2 * mod4(x + o) + (h if i == 0 else 1 - h))

        def ready(i):
            if i > 0:
                got(HB.at[at(1, 0)], z4r.at[a])

        return ring(
            2, ready,
            lambda i, o: HB.at[at(i, o)],
            lambda i, o, q: HB.at[at(i, o) + (q,)],
            xat[1], xat[3], hs.at[a], hr.at[a],
        )

    gx, gg = gather(0), gather(1)
    for a in range(2):
        for k in (1, 2, 3):
            put(XG.at[a, chip, c], XG.at[a, chip, c], zs.at[a, k], zr.at[a, k], zat[4 - k])
        if a == 0:
            next(gx)

    def cross(a):
        mine = XG.at[a, chip, c]
        there = XS.at[a, 2 * dp + lax.rem(l, 2), c]
        return copy(mine, there, ps.at[a], pr, dev(y, 1 - h, x, 2 * a + lax.rem(l, 2), c))

    @pl.when(crossing == 1)
    def _():
        cross(0).start()
        cross(1).start()

    def turn_gain(j, _):
        row = jnp.broadcast_to(gain[pl.ds(j, 1), :], (128, 128))
        GB[j // 3, pl.ds(pl.multiple_of(lax.rem(j, 3) * 128, 128), 128), :] = row.T
        return 0

    lax.fori_loop(0, 48, turn_gain, 0)
    load_wi.wait()

    def turn(j, _):
        WT[j] = WI[j].T.reshape(2, 2, 96, HID)
        return 0

    def stats(i):
        def one(o, _):
            j = mod4(y + o) * 4 + mod4(l + i)
            v = XG[0, j].reshape(CHIP, TOK).astype(F32)
            m = jnp.sum(v, axis=0, keepdims=True) * (1.0 / CHIP)
            e = v - m
            SM[pl.ds(4 * i + o, 1), :] = m
            SV[pl.ds(4 * i + o, 1), :] = jnp.sum(e * e, axis=0, keepdims=True)
            return 0

        lax.fori_loop(0, 4, one, 0)

    for t in range(6):
        if t < 4:
            lax.fori_loop(4 * t, 4 * t + 4, turn, 0)
        i = next(gx)
        if i is not None:
            stats(i)

    def exchange(a):
        for b in range(2):
            for o in (1, 3, 2):
                put(
                    XG.at[a, mod4(x + o) * 4 + 2 * h + b, c], XS.at[a, 2 * dp + b, c],
                    xs.at[a, b, o], xr.at[a, b, o], xat[o],
                )

    def own_slice(a):
        return pltpu.make_async_copy(
            XG.at[a, pl.ds(x * 4 + 2 * h, 2)], XS.at[a, pl.ds(2 * dp, 2)], loc.at[19 + a]
        )

    exchange(0)
    own_slice(0).start()
    next(gg)
    means = SM[...]
    mean = jnp.sum(means, axis=0, keepdims=True) * (1.0 / 16)
    off = means - mean
    spread = jnp.sum(SV[...], axis=0, keepdims=True) + CHIP * jnp.sum(off * off, axis=0, keepdims=True)
    inv = lax.rsqrt(spread * (1.0 / D) + 1e-06)
    ST[dp] = jnp.where(lax.broadcasted_iota(jnp.int32, (8, TOK), 0) == 0, mean, inv)
    for o in range(1, 8):
        put(ST.at[dp], ST.at[dp], sts.at[o], str_.at[o], dpat[o])

    def normalise(v, m, r, j):
        return ((v.astype(F32) - m) * r * wide(GB[j])).astype(BF16)

    PRE[...] = jnp.zeros_like(PRE)

    def pre_step(j, _):
        normed = normalise(XG[0, j].reshape(CHIP, TOK), ST[dp, 0:1, :], ST[dp, 1:2, :], j)
        PRE[...] += dot(WT[j].reshape(HID, CHIP), normed)
        return 0

    lax.fori_loop(0, 8, pre_step, 0)
    next(gg)
    lax.fori_loop(8, 16, pre_step, 0)

    pre = PRE[...]
    tanh = jnp.tanh(COEF * (pre + 0.044715 * pre * pre * pre))
    HB[0, dp] = (0.5 * pre * (1.0 + tanh)).astype(BF16).reshape(2, 192, TOK)
    PRE[...] = 0.5 * (1.0 + tanh) + 0.5 * pre * (1.0 - tanh * tanh) * COEF * (1.0 + 3.0 * 0.044715 * pre * pre)

    def over(a):
        put(HB.at[a, dp], HB.at[a, dp], z4s.at[a], z4r.at[a], opposite)

    over(0)
    ha, hg, sl = hidden_ring(0), hidden_ring(1), slices()
    next(ha)

    ACT[...] = jnp.zeros_like(ACT)
    for j in range(16):
        load_wo(j).wait()

    got(XS.at[slice_at(0, 0, c)], pr)
    for k in (1, 2, 3):
        put(XS.at[slice_at(0, 0, c)], XS.at[slice_at(0, 0, c)], z2s.at[k], z2r.at[k], zat[4 - k])

    for t in range(5):
        i = next(gg)
        if i is not None:
            def act_step(o, _):
                j = mod4(y + o) * 4 + mod4(l + i)
                ACT[...] += dot(WO[j], XG[1, j].reshape(CHIP, TOK))
                return 0

            lax.fori_loop(0, 4, act_step, 0)

    HB[1, dp] = (ACT[...] * PRE[...]).astype(BF16).reshape(2, 192, TOK)
    over(1)
    next(hg)
    exchange(1)
    own_slice(1).start()

    def partial(o):
        def one(q, _):
            j = mod4(y + o) * 4 + q
            part = dot(WI[j], HB[1, dp].reshape(HID, TOK))
            WT[j] = part.astype(BF16).reshape(2, 2, 96, TOK)
            copy(WT.at[j, 1 - c], R1.at[j], r1s.at[o, q], r1r.at[o, q], sib).start()
            return 0

        lax.fori_loop(0, 4, one, 0)

    def both(j, o, q):
        got(R1.at[j], r1r.at[o, q])
        return WT[j, c].astype(F32) + R1[j].astype(F32)

    for o in (2, 1, 3, 0):
        partial(o)
    next(ha)

    def far(q, _):
        j = mod4(y + 2) * 4 + q
        WT[j, c] = both(j, 2, q).astype(BF16)
        copy(WT.at[j, c, 0], R2.at[0, q], r2s.at[0, q], r2r.at[0, q], yat[1]).start()
        copy(WT.at[j, c, 1], R2.at[1, q], r2s.at[1, q], r2r.at[1, q], yat[3]).start()
        return 0

    lax.fori_loop(0, 4, far, 0)
    next(sl)

    def near(q, _):
        for o, w in ((1, 0), (3, 1)):
            j = mod4(y + o) * 4 + q
            total = both(j, o, q)
            got(R2.at[w, q], r2r.at[w, q])
            WT[j, c, w] = (total[w] + R2[w, q].astype(F32)).astype(BF16)
            WT[j, c, 1 - w] = total[1 - w].astype(BF16)
            copy(WT.at[j, c], R3.at[w, q], r3s.at[w, q], r3r.at[w, q], yat[o]).start()
        return 0

    lax.fori_loop(0, 4, near, 0)
    next(sl)
    next(hg)
    next(ha)

    def collect(k):
        q = mod4(l + k)
        j = y * 4 + q
        got(R3.at[0, q], r3r.at[0, q])
        got(R3.at[1, q], r3r.at[1, q])
        return both(j, 0, q) + R3[0, q].astype(F32) + R3[1, q].astype(F32)

    for k in (1, 2, 3):
        j = y * 4 + mod4(l + k)
        WT[j, c] = collect(k).astype(BF16)
        put(WT.at[j, c], R4.at[k], r4s.at[k], r4r.at[k], zat[k])
    TS[...] = collect(0)
    next(sl)
    next(hg)
    next(ha)
    for k in (1, 2, 3):
        got(R4.at[k], r4r.at[k])

    ng = TS[...] + R4[1].astype(F32) + R4[2].astype(F32) + R4[3].astype(F32) + attn[...].astype(F32)
    ng = ng.reshape(ROWS, TOK)
    own_gain = wide(GB[chip, pl.ds(pl.multiple_of(c * ROWS, ROWS), ROWS), :])
    xhat = (XG[0, chip, c].reshape(ROWS, TOK).astype(F32) - ST[dp, 0:1, :]) * ST[dp, 1:2, :]
    scaled = ng * own_gain
    s1 = jnp.sum(scaled, axis=0, keepdims=True)
    s2 = jnp.sum(scaled * xhat, axis=0, keepdims=True)
    MO[0] = jnp.where(lax.broadcasted_iota(jnp.int32, (8, TOK), 0) == 0, s1, s2)
    put(MO.at[0], MO.at[1], mos.at[0], mor.at[0], sib)
    prod = ng * xhat
    prod = prod[:, 0:128] + prod[:, 128:256] + prod[:, 256:384]
    prod = jnp.concatenate([prod, jnp.zeros((64, 128), F32)], axis=0).T
    GP[dp] = jnp.broadcast_to(jnp.sum(prod, axis=0, keepdims=True), (8, 256))
    for o in range(1, 8):
        put(GP.at[dp], GP.at[dp], gps.at[o], gpr.at[o], dpat[o])
    got(MO.at[1], mor.at[0])
    MO[2] = MO[0] + MO[1]
    for o in (1, 2, 3):
        put(MO.at[2], MO.at[2 + o], mos.at[o], mor.at[o], yat[o])
    next(sl)
    next(hg)
    for o in (1, 2, 3):
        got(MO.at[2 + o], mor.at[o])
    MO[6] = MO[2] + MO[3] + MO[4] + MO[5]
    for o in (1, 2, 3):
        put(MO.at[6], MO.at[6 + o], mos.at[3 + o], mor.at[3 + o], zat[o])

    for a in range(2):
        for b in range(2):
            for o in (1, 3, 2):
                at = XS.at[a, 2 * (2 * mod4(x + 4 - o) + h) + b, c]
                got(at, xr.at[a, b, o])
                put(at, at, xbs.at[a, b, o], xbr.at[a, b, o], sib)

    for o in (1, 2, 3):
        got(MO.at[6 + o], mor.at[3 + o])
    sums = (MO[6] + MO[7] + MO[8] + MO[9]) * (1.0 / D)
    xhat = (XG[0, chip, c].reshape(ROWS, TOK).astype(F32) - ST[dp, 0:1, :]) * ST[dp, 1:2, :]
    dx_out[...] = (
        XG[1, chip, c].reshape(ROWS, TOK).astype(F32)
        + (scaled - sums[0:1, :] - xhat * sums[1:2, :]) * ST[dp, 1:2, :]
    ).astype(BF16)

    for o in range(1, 8):
        got(GP.at[lax.rem(dp + 8 - o, 8)], gpr.at[o])
    total = GP[0]
    for o in range(1, 8):
        total = total + GP[o]
    gg_out[...] = total[0:1, 0:ROWS]

    for o in range(1, 8):
        got(ST.at[lax.rem(dp + 8 - o, 8)], str_.at[o])
    for a in range(2):
        own_slice(a).wait()
        for b in range(2):
            for o in (1, 3, 2):
                got(XS.at[a, 2 * (2 * mod4(x + 4 - o) + h) + b, 1 - c], xbr.at[a, b, o])

    dwin_out[...] = jnp.zeros_like(dwin_out)
    dwout_out[...] = jnp.zeros_like(dwout_out)

    def norm_of(d):
        for b in range(2):
            XN[2 * d + b] = normalise(
                XS[0, 2 * d + b].reshape(CHIP, TOK), ST[d, 0:1, :], ST[d, 1:2, :], 2 * dp + b
            )

    def half_sum(hh):
        def one(o, _):
            d = 2 * mod4(x + o) + hh
            norm_of(d)
            for b in range(2):
                dwin_out[pl.ds(b * CHIP, CHIP), :] += dot_nt(XN[2 * d + b], HB[1, d].reshape(HID, TOK))
                dwout_out[:, pl.ds(b * CHIP, CHIP)] += dot_nt(
                    HB[0, d].reshape(HID, TOK), XS[1, 2 * d + b].reshape(CHIP, TOK)
                )
            return 0

        lax.fori_loop(0, 4, one, 0)

    for g in (ha, hg):
        for _ in g:
            pass
    half_sum(h)
    for _ in sl:
        pass
    half_sum(1 - h)

    for made in sends:
        made.wait_send()

    @pl.when(crossing == 1)
    def _():
        cross(0).wait_send()
        cross(1).wait_send()

    def left(q, _):
        for o in range(4):
            j = mod4(y + o) * 4 + q
            copy(WT.at[j, 1 - c], R1.at[j], r1s.at[o, q], r1r.at[o, q], sib).wait_send()
        j = mod4(y + 2) * 4 + q
        copy(WT.at[j, c, 0], R2.at[0, q], r2s.at[0, q], r2r.at[0, q], yat[1]).wait_send()
        copy(WT.at[j, c, 1], R2.at[1, q], r2s.at[1, q], r2r.at[1, q], yat[3]).wait_send()
        for o, w in ((1, 0), (3, 1)):
            j = mod4(y + o) * 4 + q
            copy(WT.at[j, c], R3.at[w, q], r3s.at[w, q], r3r.at[w, q], yat[o]).wait_send()
        return 0

    lax.fori_loop(0, 4, left, 0)


def on_device(block_input, output_gradient, attn_grad, layernorm_gain, w_in, w_out):
    vmem, anywhere = pl.BlockSpec(memory_space=pltpu.VMEM), pl.BlockSpec(memory_space=pl.ANY)
    dma = pltpu.SemaphoreType.DMA
    pair = lambda *shape: [dma(shape), dma(shape)]
    scratch = [
        pltpu.VMEM((2, 16, 2, 2, 96, TOK), BF16),
        pltpu.VMEM((2, 16, 2, 2, 96, TOK), BF16),
        pltpu.VMEM((16, CHIP, TOK), BF16),
        pltpu.VMEM((16, CHIP, HID), BF16),
        pltpu.VMEM((16, 2, 2, 96, TOK), BF16),
        pltpu.VMEM((16, HID, CHIP), BF16),
        pltpu.VMEM((2, 8, 2, 192, TOK), BF16),
        pltpu.VMEM((16, CHIP, 128), F32),
        pltpu.VMEM((HID, TOK), F32),
        pltpu.VMEM((HID, TOK), F32),
        pltpu.VMEM((16, TOK), F32),
        pltpu.VMEM((16, TOK), F32),
        pltpu.VMEM((8, 8, TOK), F32),
        pltpu.VMEM((16, 2, 96, TOK), BF16),
        pltpu.VMEM((2, 4, 96, TOK), BF16),
        pltpu.VMEM((2, 4, 2, 96, TOK), BF16),
        pltpu.VMEM((4, 2, 96, TOK), BF16),
        pltpu.VMEM((2, 96, TOK), F32),
        pltpu.VMEM((10, 8, TOK), F32),
        pltpu.VMEM((8, 8, 256), F32),
    ]
    scratch += pair(2, 4) + pair(2, 4, 8) + pair(4) + pair(4, 8) + [dma((2,)), dma]
    scratch += pair(2, 2, 4) + pair(2) + pair(2, 2, 4) + pair(2, 2, 4)
    scratch += pair(4, 4) + pair(2, 4) + pair(2, 4) + pair(4) + pair(8) + pair(7) + pair(8) + [dma((21,))]
    dx, dgain, dw_in, dw_out = pl.pallas_call(
        kernel,
        out_shape=(
            jax.ShapeDtypeStruct((ROWS, TOK), BF16),
            jax.ShapeDtypeStruct((1, ROWS), F32),
            jax.ShapeDtypeStruct((768, HID), F32),
            jax.ShapeDtypeStruct((HID, 768), F32),
        ),
        in_specs=[anywhere, anywhere, vmem, vmem, anywhere, anywhere],
        out_specs=(vmem,) * 4,
        scratch_shapes=scratch,
        compiler_params=pltpu.CompilerParams(
            collective_id=0, has_side_effects=True, vmem_limit_bytes=62 * 2**20
        ),
        cost_estimate=pl.CostEstimate(flops=9 * 10**9, bytes_accessed=12 * 10**6, transcendentals=147456),
        name="parallel_block_backward",
    )(
        block_input.T.reshape(2, 96, TOK),
        output_gradient.T.reshape(2, 96, TOK),
        attn_grad.T.reshape(2, 96, TOK),
        layernorm_gain.reshape(48, 128),
        w_in.reshape(16, CHIP, HID),
        w_out,
    )
    return dx.T, dgain.reshape(ROWS), dw_in, dw_out


def solution(mesh):
    token = P("dp", "tensor")
    return jax.shard_map(
        on_device,
        mesh=mesh,
        in_specs=(token, token, token, P(), P(None, "tensor"), P("tensor", None)),
        out_specs=(token, P("tensor"), P("dp", "tensor"), P("tensor", "dp")),
        check_vma=False,
    )
```

time: 586 us -> 155 us (0.26)
  the two profiles are of different devices: /device:TPU:97 before, /device:TPU:1 now
where the time goes in v1:
time: 155 us; the launch traced here: 154 us
  Pallas kernels  147 us (95%)
  local copies, waits for them, and re-layouts  6.24 us (4%)
    pallas_call x1, Pallas kernels, on_device(): pl.pallas_call(kernel, out_shape=(jax.ShapeDtypeStruct((ROWS, TOK), BF16)...  147 us
    unnamed x6, local copies, waits for them, and re-layouts  6.24 us

profile of v1, /device:TPU:1, one launch (start us, length us, event | category | flops | bytes accessed | tf_op | source)
XLA Modules:
  0.0 154.4 jit_solution(1727301966340944591)
XLA Ops:
  0.6 147.5 %parallel_block_backward.1 = (bf16[192,384]{1,0:T(8,128)(2,1)}, f32[1,192]{1,0:T(1,128)}, f32[768,384]{1,0:T(8,128)}, f32[384,768]{1,0:T(8,128)}) custom-call(bf16[2,96,384]{2,1,0:T(8,128)(2,1)} %bitcast.16, bf16[2,96,384]{2,1,0:T(8,128)(2,1)} %bitcast.17, bf16[2,96,384]{2,1,0:T(8,128)(2,1)} %bitcast.18, f32[48,128]{1,0:T(8,128)} %bitcast.19, ...), custom_call_target="tpu_custom_call" | custom-call | flops 8999999488 | bytes 12000000 | tf_op jit(solution)/shard_map/parallel_block_backward/pallas_call | solution.py:509
  148.1 1.6 %copy.14 = bf16[384,192]{0,1:T(8,128)(2,1)} copy(bf16[384,192]{0,1:T(8,128)(2,1)} %bitcast.13) | data formatting | bytes 294912
  149.7 1.2 copy.15
  150.9 0.0 copy-start
  150.9 2.5 %copy.16 = f32[768,384]{1,0:T(8,128)} copy(f32[768,384]{1,0:T(8,128)} %get-tuple-element.18) | data formatting | bytes 2359296
  153.4 0.0 copy-done
  153.4 1.0 copy.17
Async XLA Ops:
  150.9 2.5 %copy-start = (f32[384,768]{1,0:T(8,128)S(1)}, f32[384,768]{1,0:T(8,128)}, u32[]{:S(2)}) copy-start(f32[384,768]{1,0:T(8,128)} %get-tuple-element.19) | copy-start | bytes 3538948

commit v2 on v1

--- a/solution.py
+++ b/solution.py
@@ -35,8 +35,8 @@
 def kernel(
     x_in, g_in, attn, gain, w_in, w_out,
     dx_out, gg_out, dwin_out, dwout_out,
-    XG, XS, XN, WI, WT, WO, HB, GB, PRE, ACT, SM, SV, ST, R1, R2, R3, R4, TS, MO, GP,
-    zs, zr, as_, ar, z2s, z2r, a2s, a2r, ps, pr, hs, hr, z4s, z4r, xs, xr, xbs, xbr,
+    XG, XS, XN, WI, WT, WO, HB, GB, PRE, ACT, SL, WG, SM, SV, ST, R1, R2, R3, R4, TS, MO, GP,
+    zs, zr, as_, ar, z2s, z2r, a2s, a2r, ps, pr, hs, hr, z4s, z4r, xs, xr, xbs, xbr, half_in, line_in, x_in_, y_in_,
     r1s, r1r, r2s, r2r, r3s, r3r, r4s, r4r, sts, str_, mos, mor, gps, gpr, loc,
 ):
     dp, tensor = lax.axis_index("dp"), lax.axis_index("tensor")
@@ -74,8 +74,16 @@
         copy(dst, dst, recv, recv, sib).wait_recv()
 
     barrier = pltpu.get_barrier_semaphore()
-    for to in [sib] + yat[1:] + zat[1:] + dpat[1:] + [dev(y, 1 - h, x, 2 * h + lax.rem(l, 2), c)]:
+    for to in [sib] + yat[1:] + zat[1:] + xat[1:]:
         pl.semaphore_signal(barrier, inc=1, device_id=to, device_id_type=MESH)
+
+    @pl.when(l == 0)
+    def _():
+        pl.semaphore_signal(barrier, inc=1, device_id=dev(x, 1 - h, y, 3, c), device_id_type=MESH)
+
+    @pl.when(l == 3)
+    def _():
+        pl.semaphore_signal(barrier, inc=1, device_id=dev(x, 1 - h, y, 0, c), device_id_type=MESH)
 
     own_x = pltpu.make_async_copy(x_in, XG.at[0, chip, c], loc.at[0])
     own_g = pltpu.make_async_copy(g_in, XG.at[1, chip, c], loc.at[1])
@@ -91,7 +99,32 @@
         load_wo(j).start()
     own_x.wait()
     own_g.wait()
-    pl.semaphore_wait(barrier, 14 + 2 * crossing)
+    pl.semaphore_wait(barrier, jnp.where(lax.rem(l, 3) == 0, 11, 10))
+
+    @pl.when(l == 0)
+    def _():
+        pl.semaphore_signal(half_in, inc=1, device_id=dev(x, 1 - h, y, 3, c), device_id_type=MESH)
+
+    def pass_on(step):
+        if step == 0:
+            @pl.when(l == 3)
+            def _():
+                pl.semaphore_wait(half_in, 1)
+                for to in zat[1:]:
+                    pl.semaphore_signal(line_in, inc=1, device_id=to, device_id_type=MESH)
+        if step == 1:
+            @pl.when(l < 3)
+            def _():
+                pl.semaphore_wait(line_in, 1)
+
+            for to in xat[1:]:
+                pl.semaphore_signal(x_in_, inc=1, device_id=to, device_id_type=MESH)
+        if step == 2:
+            pl.semaphore_wait(x_in_, 3)
+            for to in yat[1:]:
+                pl.semaphore_signal(y_in_, inc=1, device_id=to, device_id_type=MESH)
+        if step == 3:
+            pl.semaphore_wait(y_in_, 3)
 
     def ring(n, ready, view, half, plus, minus, ss, rs, other=None):
         def first(i):
@@ -122,42 +155,68 @@
                     got(other(i, o), rs.at[i, 4 + o])
 
         for t in range(n + 3):
-            if t < n:
+            if t < n and other:
                 first(t)
+                yield None
             if 0 <= t - 1 < n:
                 second(t - 1)
+                yield None
+            if t < n and not other:
+                first(t)
+                yield None
             if 0 <= t - 2 < n:
                 third(t - 2)
+                yield None
             if 0 <= t - 3 < n:
                 last(t - 3)
-                yield t - 3
-            else:
-                yield None
+            yield t
 
     def chip_at(i, o):
         return mod4(y + o) * 4 + mod4(l + i)
 
-    def gather(a):
+    queue = [(a, k) for a in range(2) for k in (1, 2, 3)]
+
+    def along_z(count):
+        for a, k in queue[:count]:
+            put(XG.at[a, chip, c], XG.at[a, chip, c], zs.at[a, k], zr.at[a, k], zat[4 - k])
+        del queue[:count]
+
+    order = [(0, 0), (1, 0), (0, 1), (0, 2), (0, 3), (1, 1), (1, 2), (1, 3)]
+
+    def gather():
+        def block(i, o, c_):
+            a, k = order[i]
+            return XG.at[a, chip_at(k, o), c_]
+
         def ready(i):
+            a, k = order[i]
+            if k > 0:
+                got(block(i, 0, c), zr.at[a, k])
             if i > 0:
-                got(XG.at[a, chip_at(i, 0), c], zr.at[a, i])
+                along_z(1)
 
         return ring(
-            4, ready,
-            lambda i, o: XG.at[a, chip_at(i, o), c],
-            lambda i, o, q: XG.at[a, chip_at(i, o), c, q],
-            yat[1], yat[3], as_.at[a], ar.at[a],
-            lambda i, o: XG.at[a, chip_at(i, o), 1 - c],
+            8, ready,
+            lambda i, o: block(i, o, c),
+            lambda i, o, q: XG.at[order[i][0], chip_at(order[i][1], o), c, q],
+            yat[1], yat[3], as_, ar,
+            lambda i, o: block(i, o, 1 - c),
         )
 
     def slice_at(i, o, c_):
         lp = mod4(l + i)
         return (lp // 2, 2 * (2 * mod4(y + o) + (1 - h)) + lax.rem(lp, 2), c_)
+
+    def slice_along_z(ks):
+        for k in ks:
+            put(XS.at[slice_at(0, 0, c)], XS.at[slice_at(0, 0, c)], z2s.at[k], z2r.at[k], zat[4 - k])
 
     def slices():
         def ready(i):
             if i > 0:
                 got(XS.at[slice_at(i, 0, c)], z2r.at[i])
+            if i == 1:
+                slice_along_z((3,))
 
         return ring(
             4, ready,
@@ -182,29 +241,34 @@
             xat[1], xat[3], hs.at[a], hr.at[a],
         )
 
-    gx, gg = gather(0), gather(1)
-    for a in range(2):
-        for k in (1, 2, 3):
-            put(XG.at[a, chip, c], XG.at[a, chip, c], zs.at[a, k], zr.at[a, k], zat[4 - k])
-        if a == 0:
-            next(gx)
+    tok = gather()
+    def step(ring_, t, between=None):
+        while True:
+            at = next(ring_, t)
+            if at == t:
+                return
+            if between is not None:
+                between()
+
+    along_z(2)
+    step(tok, 0)
 
     def cross(a):
         mine = XG.at[a, chip, c]
         there = XS.at[a, 2 * dp + lax.rem(l, 2), c]
         return copy(mine, there, ps.at[a], pr, dev(y, 1 - h, x, 2 * a + lax.rem(l, 2), c))
 
-    @pl.when(crossing == 1)
-    def _():
-        cross(0).start()
-        cross(1).start()
+    def cross_over():
+        @pl.when(crossing == 1)
+        def _():
+            cross(0).start()
+            cross(1).start()
 
     def turn_gain(j, _):
         row = jnp.broadcast_to(gain[pl.ds(j, 1), :], (128, 128))
         GB[j // 3, pl.ds(pl.multiple_of(lax.rem(j, 3) * 128, 128), 128), :] = row.T
         return 0
 
-    lax.fori_loop(0, 48, turn_gain, 0)
     load_wi.wait()
 
     def turn(j, _):
@@ -221,31 +285,90 @@
             SV[pl.ds(4 * i + o, 1), :] = jnp.sum(e * e, axis=0, keepdims=True)
             return 0
 
-        lax.fori_loop(0, 4, one, 0)
-
-    for t in range(6):
-        if t < 4:
-            lax.fori_loop(4 * t, 4 * t + 4, turn, 0)
-        i = next(gx)
-        if i is not None:
-            stats(i)
-
-    def exchange(a):
+        lax.fori_loop(0, 4, one, 0, unroll=2)
+
+    def share(a, i):
+        lp = mod4(l + i)
+        b = lax.rem(lp, 2)
+
+        @pl.when(lp // 2 == h)
+        def _():
+            for o in (1, 3, 2):
+                copy(
+                    XG.at[a, mod4(x + o) * 4 + lp, c], XS.at[a, 2 * dp + b, c],
+                    xs.at[a, b, o], xr.at[a, b, o], xat[o],
+                ).start()
+
+    def relay(a):
         for b in range(2):
             for o in (1, 3, 2):
-                put(
-                    XG.at[a, mod4(x + o) * 4 + 2 * h + b, c], XS.at[a, 2 * dp + b, c],
-                    xs.at[a, b, o], xr.at[a, b, o], xat[o],
-                )
+                at = XS.at[a, 2 * (2 * mod4(x + 4 - o) + h) + b, c]
+                got(at, xr.at[a, b, o])
+                put(at, at, xbs.at[a, b, o], xbr.at[a, b, o], sib)
+
+    def relayed(a):
+        own_slice(a).wait()
+        for b in range(2):
+            for o in (1, 3, 2):
+                got(XS.at[a, 2 * (2 * mod4(x + 4 - o) + h) + b, 1 - c], xbr.at[a, b, o])
 
     def own_slice(a):
         return pltpu.make_async_copy(
             XG.at[a, pl.ds(x * 4 + 2 * h, 2)], XS.at[a, pl.ds(2 * dp, 2)], loc.at[19 + a]
         )
 
-    exchange(0)
+    def gain_step(j, _):
+        g = GB[j]
+        high = g.astype(BF16)
+        low = (g - high.astype(F32)).astype(BF16)
+        w = WT[j].reshape(HID, CHIP)
+        WG[...] += dot(w, high) + dot(w, low)
+        return 0
+
+    def act_step(i):
+        def one(o, _):
+            j = mod4(y + o) * 4 + mod4(l + i)
+            ACT[...] += dot(WO[j], XG[1, j].reshape(CHIP, TOK))
+            return 0
+
+        lax.fori_loop(0, 4, one, 0, unroll=True)
+
+    WG[...] = jnp.zeros_like(WG)
+    ACT[...] = jnp.zeros_like(ACT)
+    pass_on(0)
+    lax.fori_loop(0, 8, turn, 0, unroll=2)
+    pass_on(1)
+    lax.fori_loop(0, 12, turn_gain, 0, unroll=4)
+    step(tok, 1)
+    pass_on(2)
+    lax.fori_loop(8, 16, turn, 0, unroll=2)
+    lax.fori_loop(12, 24, turn_gain, 0, unroll=4)
+    step(tok, 2)
+    share(0, 0)
+    pass_on(3)
+    cross_over()
+    lax.fori_loop(24, 48, turn_gain, 0, unroll=4)
+    step(tok, 3)
+    share(1, 0)
+    stats(0)
+    step(tok, 4)
+    share(0, 1)
+    for j in range(16):
+        load_wo(j).wait()
+    lax.fori_loop(0, 8, gain_step, 0, unroll=2)
+    step(tok, 5)
+    share(0, 2)
+    stats(1)
+    lax.fori_loop(8, 16, gain_step, 0, unroll=2)
+    step(tok, 6)
+    share(0, 3)
+    stats(2)
+    act_step(0)
+    step(tok, 7)
+    share(1, 1)
+    stats(3)
+
     own_slice(0).start()
-    next(gg)
     means = SM[...]
     mean = jnp.sum(means, axis=0, keepdims=True) * (1.0 / 16)
     off = means - mean
@@ -265,65 +388,90 @@
         PRE[...] += dot(WT[j].reshape(HID, CHIP), normed)
         return 0
 
-    lax.fori_loop(0, 8, pre_step, 0)
-    next(gg)
-    lax.fori_loop(8, 16, pre_step, 0)
+    pieces = [lambda b=b: lax.fori_loop(4 * b, 4 * b + 4, pre_step, 0, unroll=True) for b in range(4)]
+
+    def piece():
+        if pieces:
+            pieces.pop(0)()
+
+    piece()
+    step(tok, 8, piece)
+    while pieces:
+        piece()
 
     pre = PRE[...]
     tanh = jnp.tanh(COEF * (pre + 0.044715 * pre * pre * pre))
     HB[0, dp] = (0.5 * pre * (1.0 + tanh)).astype(BF16).reshape(2, 192, TOK)
-    PRE[...] = 0.5 * (1.0 + tanh) + 0.5 * pre * (1.0 - tanh * tanh) * COEF * (1.0 + 3.0 * 0.044715 * pre * pre)
+    SL[...] = 0.5 * (1.0 + tanh) + 0.5 * pre * (1.0 - tanh * tanh) * COEF * (1.0 + 3.0 * 0.044715 * pre * pre)
 
     def over(a):
         put(HB.at[a, dp], HB.at[a, dp], z4s.at[a], z4r.at[a], opposite)
 
     over(0)
     ha, hg, sl = hidden_ring(0), hidden_ring(1), slices()
-    next(ha)
-
-    ACT[...] = jnp.zeros_like(ACT)
-    for j in range(16):
-        load_wo(j).wait()
-
+    step(ha, 0)
+    share(1, 2)
     got(XS.at[slice_at(0, 0, c)], pr)
-    for k in (1, 2, 3):
-        put(XS.at[slice_at(0, 0, c)], XS.at[slice_at(0, 0, c)], z2s.at[k], z2r.at[k], zat[4 - k])
-
-    for t in range(5):
-        i = next(gg)
-        if i is not None:
-            def act_step(o, _):
-                j = mod4(y + o) * 4 + mod4(l + i)
-                ACT[...] += dot(WO[j], XG[1, j].reshape(CHIP, TOK))
-                return 0
-
-            lax.fori_loop(0, 4, act_step, 0)
-
-    HB[1, dp] = (ACT[...] * PRE[...]).astype(BF16).reshape(2, 192, TOK)
+    slice_along_z((1, 2))
+    act_step(1)
+    step(tok, 9)
+    share(1, 3)
+    step(sl, 0)
+    act_step(2)
+    relay(0)
+    step(tok, 10)
+    act_step(3)
+
+    HB[1, dp] = (ACT[...] * SL[...]).astype(BF16).reshape(2, 192, TOK)
     over(1)
-    next(hg)
-    exchange(1)
+    step(hg, 0)
     own_slice(1).start()
 
+    own_gain = wide(GB[chip, pl.ds(pl.multiple_of(c * ROWS, ROWS), ROWS), :])
+
+    def own_xhat():
+        return (XG[0, chip, c].reshape(ROWS, TOK).astype(F32) - ST[dp, 0:1, :]) * ST[dp, 1:2, :]
+
+    def row_sums():
+        grad = HB[1, dp].reshape(HID, TOK).astype(F32)
+        side = attn[...].reshape(ROWS, TOK).astype(F32) * own_gain
+        s1 = jnp.sum(grad * wide(WG[...]), axis=0, keepdims=True) + jnp.sum(side, axis=0, keepdims=True)
+        s2 = jnp.sum(grad * PRE[...], axis=0, keepdims=True) + jnp.sum(side * own_xhat(), axis=0, keepdims=True)
+        MO[0] = jnp.where(lax.broadcasted_iota(jnp.int32, (8, TOK), 0) == 0, s1, s2)
+        put(MO.at[0], MO.at[1], mos.at[0], mor.at[0], sib)
+
+    def row_sums_y():
+        got(MO.at[1], mor.at[0])
+        MO[2] = MO[0] + MO[1]
+        for o in (1, 2, 3):
+            put(MO.at[2], MO.at[2 + o], mos.at[o], mor.at[o], yat[o])
+
+    def row_sums_z():
+        for o in (1, 2, 3):
+            got(MO.at[2 + o], mor.at[o])
+        MO[6] = MO[2] + MO[3] + MO[4] + MO[5]
+        for o in (1, 2, 3):
+            put(MO.at[6], MO.at[6 + o], mos.at[3 + o], mor.at[3 + o], zat[o])
+
     def partial(o):
-        def one(q, _):
+        def one(n, _):
+            q = mod4(l + 1 + n)
             j = mod4(y + o) * 4 + q
             part = dot(WI[j], HB[1, dp].reshape(HID, TOK))
             WT[j] = part.astype(BF16).reshape(2, 2, 96, TOK)
             copy(WT.at[j, 1 - c], R1.at[j], r1s.at[o, q], r1r.at[o, q], sib).start()
             return 0
 
-        lax.fori_loop(0, 4, one, 0)
+        lax.fori_loop(0, 4, one, 0, unroll=True)
 
     def both(j, o, q):
         got(R1.at[j], r1r.at[o, q])
         return WT[j, c].astype(F32) + R1[j].astype(F32)
 
-    for o in (2, 1, 3, 0):
-        partial(o)
-    next(ha)
-
-    def far(q, _):
+    partial(2)
+    partial(1)
+    def far(n, _):
+        q = mod4(l + 1 + n)
         j = mod4(y + 2) * 4 + q
         WT[j, c] = both(j, 2, q).astype(BF16)
         copy(WT.at[j, c, 0], R2.at[0, q], r2s.at[0, q], r2r.at[0, q], yat[1]).start()
@@ -331,9 +479,14 @@
         return 0
 
     lax.fori_loop(0, 4, far, 0)
-    next(sl)
-
-    def near(q, _):
+    partial(3)
+    row_sums()
+    partial(0)
+    step(sl, 1)
+    row_sums_y()
+
+    def near(n, _):
+        q = mod4(l + 1 + n)
         for o, w in ((1, 0), (3, 1)):
             j = mod4(y + o) * 4 + q
             total = both(j, o, q)
@@ -344,9 +497,48 @@
         return 0
 
     lax.fori_loop(0, 4, near, 0)
-    next(sl)
-    next(hg)
-    next(ha)
+
+    def norm_of(hh):
+        def one(o, _):
+            d = 2 * mod4(x + o) + hh
+            for b in range(2):
+                XN[2 * d + b] = normalise(
+                    XS[0, 2 * d + b].reshape(CHIP, TOK), ST[d, 0:1, :], ST[d, 1:2, :], 2 * dp + b
+                )
+            return 0
+
+        lax.fori_loop(0, 4, one, 0, unroll=2)
+
+    def sum_in(hh):
+        def one(o, _):
+            d = 2 * mod4(x + o) + hh
+            dwin_out[...] += dot_nt(XN[pl.ds(2 * d, 2)].reshape(768, TOK), HB[1, d].reshape(HID, TOK))
+            return 0
+
+        lax.fori_loop(0, 4, one, 0, unroll=2)
+
+    def sum_out(hh):
+        def one(o, _):
+            d = 2 * mod4(x + o) + hh
+            dwout_out[...] += dot_nt(HB[0, d].reshape(HID, TOK), XS[1, pl.ds(2 * d, 2)].reshape(768, TOK))
+            return 0
+
+        lax.fori_loop(0, 4, one, 0, unroll=2)
+
+    dwin_out[...] = jnp.zeros_like(dwin_out)
+    dwout_out[...] = jnp.zeros_like(dwout_out)
+    step(ha, 1)
+    row_sums_z()
+    relay(1)
+    step(ha, 2)
+    step(sl, 2)
+    step(hg, 1)
+    for o in range(1, 8):
+        got(ST.at[lax.rem(dp + 8 - o, 8)], str_.at[o])
+    relayed(0)
+    norm_of(h)
+    relayed(1)
+    sum_out(h)
 
     def collect(k):
         q = mod4(l + k)
@@ -360,54 +552,35 @@
         WT[j, c] = collect(k).astype(BF16)
         put(WT.at[j, c], R4.at[k], r4s.at[k], r4r.at[k], zat[k])
     TS[...] = collect(0)
-    next(sl)
-    next(hg)
-    next(ha)
+    step(sl, 3)
+    step(hg, 2)
     for k in (1, 2, 3):
         got(R4.at[k], r4r.at[k])
 
     ng = TS[...] + R4[1].astype(F32) + R4[2].astype(F32) + R4[3].astype(F32) + attn[...].astype(F32)
     ng = ng.reshape(ROWS, TOK)
-    own_gain = wide(GB[chip, pl.ds(pl.multiple_of(c * ROWS, ROWS), ROWS), :])
-    xhat = (XG[0, chip, c].reshape(ROWS, TOK).astype(F32) - ST[dp, 0:1, :]) * ST[dp, 1:2, :]
-    scaled = ng * own_gain
-    s1 = jnp.sum(scaled, axis=0, keepdims=True)
-    s2 = jnp.sum(scaled * xhat, axis=0, keepdims=True)
-    MO[0] = jnp.where(lax.broadcasted_iota(jnp.int32, (8, TOK), 0) == 0, s1, s2)
-    put(MO.at[0], MO.at[1], mos.at[0], mor.at[0], sib)
+    xhat = own_xhat()
     prod = ng * xhat
     prod = prod[:, 0:128] + prod[:, 128:256] + prod[:, 256:384]
     prod = jnp.concatenate([prod, jnp.zeros((64, 128), F32)], axis=0).T
     GP[dp] = jnp.broadcast_to(jnp.sum(prod, axis=0, keepdims=True), (8, 256))
     for o in range(1, 8):
         put(GP.at[dp], GP.at[dp], gps.at[o], gpr.at[o], dpat[o])
-    got(MO.at[1], mor.at[0])
-    MO[2] = MO[0] + MO[1]
-    for o in (1, 2, 3):
-        put(MO.at[2], MO.at[2 + o], mos.at[o], mor.at[o], yat[o])
-    next(sl)
-    next(hg)
-    for o in (1, 2, 3):
-        got(MO.at[2 + o], mor.at[o])
-    MO[6] = MO[2] + MO[3] + MO[4] + MO[5]
-    for o in (1, 2, 3):
-        put(MO.at[6], MO.at[6 + o], mos.at[3 + o], mor.at[3 + o], zat[o])
-
-    for a in range(2):
-        for b in range(2):
-            for o in (1, 3, 2):
-                at = XS.at[a, 2 * (2 * mod4(x + 4 - o) + h) + b, c]
-                got(at, xr.at[a, b, o])
-                put(at, at, xbs.at[a, b, o], xbr.at[a, b, o], sib)
-
+    step(sl, 4)
     for o in (1, 2, 3):
         got(MO.at[6 + o], mor.at[3 + o])
     sums = (MO[6] + MO[7] + MO[8] + MO[9]) * (1.0 / D)
-    xhat = (XG[0, chip, c].reshape(ROWS, TOK).astype(F32) - ST[dp, 0:1, :]) * ST[dp, 1:2, :]
     dx_out[...] = (
         XG[1, chip, c].reshape(ROWS, TOK).astype(F32)
-        + (scaled - sums[0:1, :] - xhat * sums[1:2, :]) * ST[dp, 1:2, :]
+        + (ng * own_gain - sums[0:1, :] - xhat * sums[1:2, :]) * ST[dp, 1:2, :]
     ).astype(BF16)
+    sum_in(h)
+    for g in (ha, hg, sl):
+        for _ in g:
+            pass
+    sum_out(1 - h)
+    norm_of(1 - h)
+    sum_in(1 - h)
 
     for o in range(1, 8):
         got(GP.at[lax.rem(dp + 8 - o, 8)], gpr.at[o])
@@ -416,46 +589,15 @@
         total = total + GP[o]
     gg_out[...] = total[0:1, 0:ROWS]
 
-    for o in range(1, 8):
-        got(ST.at[lax.rem(dp + 8 - o, 8)], str_.at[o])
-    for a in range(2):
-        own_slice(a).wait()
-        for b in range(2):
-            for o in (1, 3, 2):
-                got(XS.at[a, 2 * (2 * mod4(x + 4 - o) + h) + b, 1 - c], xbr.at[a, b, o])
-
-    dwin_out[...] = jnp.zeros_like(dwin_out)
-    dwout_out[...] = jnp.zeros_like(dwout_out)
-
-    def norm_of(d):
-        for b in range(2):
-            XN[2 * d + b] = normalise(
-                XS[0, 2 * d + b].reshape(CHIP, TOK), ST[d, 0:1, :], ST[d, 1:2, :], 2 * dp + b
-            )
-
-    def half_sum(hh):
-        def one(o, _):
-            d = 2 * mod4(x + o) + hh
-            norm_of(d)
-            for b in range(2):
-                dwin_out[pl.ds(b * CHIP, CHIP), :] += dot_nt(XN[2 * d + b], HB[1, d].reshape(HID, TOK))
-                dwout_out[:, pl.ds(b * CHIP, CHIP)] += dot_nt(
-                    HB[0, d].reshape(HID, TOK), XS[1, 2 * d + b].reshape(CHIP, TOK)
-                )
-            return 0
-
-        lax.fori_loop(0, 4, one, 0)
-
-    for g in (ha, hg):
-        for _ in g:
-            pass
-    half_sum(h)
-    for _ in sl:
-        pass
-    half_sum(1 - h)
-
     for made in sends:
         made.wait_send()
+    for a in range(2):
+        for b in range(2):
+            for o in (1, 2, 3):
+                copy(
+                    XG.at[a, mod4(x + o) * 4 + 2 * h + b, c], XS.at[a, 2 * dp + b, c],
+                    xs.at[a, b, o], xr.at[a, b, o], xat[o],
+                ).wait_send()
 
     @pl.when(crossing == 1)
     def _():
@@ -475,6 +617,19 @@
         return 0
 
     lax.fori_loop(0, 4, left, 0)
+
+
+def hand_over(*refs):
+    sources, results, between, sems = refs[:4], refs[4:8], refs[8:12], refs[12]
+    arrive = [pltpu.make_async_copy(a, b, sems.at[0, i]) for i, (a, b) in enumerate(zip(sources, between))]
+    leave = [pltpu.make_async_copy(a, b, sems.at[1, i]) for i, (a, b) in enumerate(zip(between, results))]
+    for made in arrive:
+        made.start()
+    for one, two in zip(arrive, leave):
+        one.wait()
+        two.start()
+    for made in leave:
+        made.wait()
 
 
 def on_device(block_input, output_gradient, attn_grad, layernorm_gain, w_in, w_out):
@@ -492,6 +647,8 @@
         pltpu.VMEM((16, CHIP, 128), F32),
         pltpu.VMEM((HID, TOK), F32),
         pltpu.VMEM((HID, TOK), F32),
+        pltpu.VMEM((HID, TOK), F32),
+        pltpu.VMEM((HID, 128), F32),
         pltpu.VMEM((16, TOK), F32),
         pltpu.VMEM((16, TOK), F32),
         pltpu.VMEM((8, 8, TOK), F32),
@@ -503,17 +660,19 @@
         pltpu.VMEM((10, 8, TOK), F32),
         pltpu.VMEM((8, 8, 256), F32),
     ]
-    scratch += pair(2, 4) + pair(2, 4, 8) + pair(4) + pair(4, 8) + [dma((2,)), dma]
+    scratch += pair(2, 4) + pair(8, 8) + pair(4) + pair(4, 8) + [dma((2,)), dma]
     scratch += pair(2, 2, 4) + pair(2) + pair(2, 2, 4) + pair(2, 2, 4)
+    scratch += [pltpu.SemaphoreType.REGULAR] * 4
     scratch += pair(4, 4) + pair(2, 4) + pair(2, 4) + pair(4) + pair(8) + pair(7) + pair(8) + [dma((21,))]
-    dx, dgain, dw_in, dw_out = pl.pallas_call(
+    shapes = (
+        jax.ShapeDtypeStruct((ROWS, TOK), BF16),
+        jax.ShapeDtypeStruct((1, ROWS), F32),
+        jax.ShapeDtypeStruct((768, HID), F32),
+        jax.ShapeDtypeStruct((HID, 768), F32),
+    )
+    results = pl.pallas_call(
         kernel,
-        out_shape=(
-            jax.ShapeDtypeStruct((ROWS, TOK), BF16),
-            jax.ShapeDtypeStruct((1, ROWS), F32),
-            jax.ShapeDtypeStruct((768, HID), F32),
-            jax.ShapeDtypeStruct((HID, 768), F32),
-        ),
+        out_shape=shapes,
         in_specs=[anywhere, anywhere, vmem, vmem, anywhere, anywhere],
         out_specs=(vmem,) * 4,
         scratch_shapes=scratch,
@@ -530,6 +689,14 @@
         w_in.reshape(16, CHIP, HID),
         w_out,
     )
+    dx, dgain, dw_in, dw_out = pl.pallas_call(
+        hand_over,
+        out_shape=shapes,
+        in_specs=[anywhere] * 4,
+        out_specs=(anywhere,) * 4,
+        scratch_shapes=[pltpu.VMEM(s.shape, s.dtype) for s in shapes] + [dma((2, 4))],
+        name="results",
+    )(*results)
     return dx.T, dgain.reshape(ROWS), dw_in, dw_out
 
 

time: 155 us -> 131 us (0.85)
  the two profiles are of different devices: /device:TPU:1 before, /device:TPU:97 now
where the time goes in v2:
time: 131 us; the launch traced here: 130 us
  Pallas kernels  129 us (98%)
    pallas_call x1, Pallas kernels, on_device(): pl.pallas_call(kernel, out_shape=shapes, in_specs=[anywhere, anywhere, vm...  126 us
    pallas_call x1, Pallas kernels, on_device(): pl.pallas_call(hand_over, out_shape=shapes, in_specs=[anywhere] * 4, out_...  2.83 us

profile of v2, /device:TPU:97, one launch (start us, length us, event | category | flops | bytes accessed | tf_op | source)
XLA Modules:
  0.0 130.1 jit_solution(15966525716251786996)
XLA Ops:
  0.6 126.5 %parallel_block_backward.1 = (bf16[192,384]{1,0:T(8,128)(2,1)}, f32[1,192]{1,0:T(1,128)}, f32[768,384]{1,0:T(8,128)}, f32[384,768]{1,0:T(8,128)}) custom-call(bf16[2,96,384]{2,1,0:T(8,128)(2,1)} %bitcast.14, bf16[2,96,384]{2,1,0:T(8,128)(2,1)} %bitcast.15, bf16[2,96,384]{2,1,0:T(8,128)(2,1)} %bitcast.16, f32[48,128]{1,0:T(8,128)} %bitcast.18, ...), custom_call_target="tpu_custom_call" | custom-call | flops 8999999488 | bytes 12000000 | tf_op jit(solution)/shard_map/parallel_block_backward/pallas_call | solution.py:673
  127.1 2.8 %results.1 = (bf16[192,384]{1,0:T(8,128)(2,1)}, f32[1,192]{1,0:T(1,128)}, f32[768,384]{1,0:T(8,128)}, f32[384,768]{1,0:T(8,128)}) custom-call(bf16[192,384]{1,0:T(8,128)(2,1)} %get-tuple-element.12.refs_0_, f32[1,192]{1,0:T(1,128)} %get-tuple-element.13.refs_1_, f32[768,384]{1,0:T(8,128)} %get-tuple-element.14.refs_2_, f32[384,768]{1,0:T(8,128)} %get-tuple-element.15.refs_3_), custom_call_target="tpu_custom_call" | custom-call | tf_op jit(solution)/shard_map/results/pallas_call | solution.py:692

commit v3 on v2

--- a/solution.py
+++ b/solution.py
@@ -181,7 +181,7 @@
             put(XG.at[a, chip, c], XG.at[a, chip, c], zs.at[a, k], zr.at[a, k], zat[4 - k])
         del queue[:count]
 
-    order = [(0, 0), (1, 0), (0, 1), (0, 2), (0, 3), (1, 1), (1, 2), (1, 3)]
+    order = [(a, k) for a in range(2) for k in range(4)]
 
     def gather():
         def block(i, o, c_):
@@ -215,8 +215,6 @@
         def ready(i):
             if i > 0:
                 got(XS.at[slice_at(i, 0, c)], z2r.at[i])
-            if i == 1:
-                slice_along_z((3,))
 
         return ring(
             4, ready,
@@ -250,7 +248,7 @@
             if between is not None:
                 between()
 
-    along_z(2)
+    along_z(1)
     step(tok, 0)
 
     def cross(a):
@@ -335,37 +333,34 @@
 
     WG[...] = jnp.zeros_like(WG)
     ACT[...] = jnp.zeros_like(ACT)
-    pass_on(0)
     lax.fori_loop(0, 8, turn, 0, unroll=2)
-    pass_on(1)
     lax.fori_loop(0, 12, turn_gain, 0, unroll=4)
     step(tok, 1)
-    pass_on(2)
     lax.fori_loop(8, 16, turn, 0, unroll=2)
     lax.fori_loop(12, 24, turn_gain, 0, unroll=4)
+    pass_on(0)
     step(tok, 2)
     share(0, 0)
-    pass_on(3)
-    cross_over()
     lax.fori_loop(24, 48, turn_gain, 0, unroll=4)
+    pass_on(1)
     step(tok, 3)
-    share(1, 0)
+    share(0, 1)
     stats(0)
-    step(tok, 4)
-    share(0, 1)
     for j in range(16):
         load_wo(j).wait()
     lax.fori_loop(0, 8, gain_step, 0, unroll=2)
-    step(tok, 5)
+    pass_on(2)
+    step(tok, 4)
     share(0, 2)
     stats(1)
     lax.fori_loop(8, 16, gain_step, 0, unroll=2)
-    step(tok, 6)
+    pass_on(3)
+    step(tok, 5)
     share(0, 3)
     stats(2)
-    act_step(0)
-    step(tok, 7)
-    share(1, 1)
+    cross_over()
+    step(tok, 6)
+    share(1, 0)
     stats(3)
 
     own_slice(0).start()
@@ -395,7 +390,7 @@
             pieces.pop(0)()
 
     piece()
-    step(tok, 8, piece)
+    step(tok, 7, piece)
     while pieces:
         piece()
 
@@ -410,15 +405,17 @@
     over(0)
     ha, hg, sl = hidden_ring(0), hidden_ring(1), slices()
     step(ha, 0)
+    share(1, 1)
+    act_step(0)
+    step(tok, 8)
     share(1, 2)
+    act_step(1)
     got(XS.at[slice_at(0, 0, c)], pr)
-    slice_along_z((1, 2))
-    act_step(1)
+    slice_along_z((1, 2, 3))
     step(tok, 9)
     share(1, 3)
     step(sl, 0)
     act_step(2)
-    relay(0)
     step(tok, 10)
     act_step(3)
 
@@ -469,7 +466,9 @@
         return WT[j, c].astype(F32) + R1[j].astype(F32)
 
     partial(2)
+    next(ha)
     partial(1)
+
     def far(n, _):
         q = mod4(l + 1 + n)
         j = mod4(y + 2) * 4 + q
@@ -482,6 +481,7 @@
     partial(3)
     row_sums()
     partial(0)
+    step(ha, 1)
     step(sl, 1)
     row_sums_y()
 
@@ -496,7 +496,9 @@
             copy(WT.at[j, c], R3.at[w, q], r3s.at[w, q], r3r.at[w, q], yat[o]).start()
         return 0
 
-    lax.fori_loop(0, 4, near, 0)
+    lax.fori_loop(0, 2, near, 0)
+    next(hg)
+    lax.fori_loop(2, 4, near, 0)
 
     def norm_of(hh):
         def one(o, _):
@@ -527,16 +529,16 @@
 
     dwin_out[...] = jnp.zeros_like(dwin_out)
     dwout_out[...] = jnp.zeros_like(dwout_out)
-    step(ha, 1)
     row_sums_z()
+    step(ha, 2)
+    relay(0)
     relay(1)
-    step(ha, 2)
     step(sl, 2)
-    step(hg, 1)
     for o in range(1, 8):
         got(ST.at[lax.rem(dp + 8 - o, 8)], str_.at[o])
     relayed(0)
     norm_of(h)
+    step(hg, 1)
     relayed(1)
     sum_out(h)
 
@@ -575,19 +577,19 @@
         + (ng * own_gain - sums[0:1, :] - xhat * sums[1:2, :]) * ST[dp, 1:2, :]
     ).astype(BF16)
     sum_in(h)
-    for g in (ha, hg, sl):
-        for _ in g:
-            pass
-    sum_out(1 - h)
-    norm_of(1 - h)
-    sum_in(1 - h)
-
+    step(sl, 5)
+    step(sl, 6)
+    step(ha, 4)
     for o in range(1, 8):
         got(GP.at[lax.rem(dp + 8 - o, 8)], gpr.at[o])
     total = GP[0]
     for o in range(1, 8):
         total = total + GP[o]
     gg_out[...] = total[0:1, 0:ROWS]
+    norm_of(1 - h)
+    sum_out(1 - h)
+    step(hg, 4)
+    sum_in(1 - h)
 
     for made in sends:
         made.wait_send()

time: 131 us -> 129 us (0.985)
    pallas_call x1, Pallas kernels: 126 us -> 125 us  [on_device(): pl.pallas_call(kernel, out_shape=shapes, in_specs=[anywhere, anywhere, vm...]
where the time goes in v3:
time: 129 us
  Pallas kernels  128 us (99%)
    pallas_call x1, Pallas kernels, on_device(): pl.pallas_call(kernel, out_shape=shapes, in_specs=[anywhere, anywhere, vm...  125 us
    pallas_call x1, Pallas kernels, on_device(): pl.pallas_call(hand_over, out_shape=shapes, in_specs=[anywhere] * 4, out_...  2.83 us

profile of v3, /device:TPU:97, one launch (start us, length us, event | category | flops | bytes accessed | tf_op | source)
XLA Modules:
  0.0 128.6 jit_solution(8288567519345976049)
XLA Ops:
  0.6 124.9 %parallel_block_backward.1 = (bf16[192,384]{1,0:T(8,128)(2,1)}, f32[1,192]{1,0:T(1,128)}, f32[768,384]{1,0:T(8,128)}, f32[384,768]{1,0:T(8,128)}) custom-call(bf16[2,96,384]{2,1,0:T(8,128)(2,1)} %bitcast.14, bf16[2,96,384]{2,1,0:T(8,128)(2,1)} %bitcast.15, bf16[2,96,384]{2,1,0:T(8,128)(2,1)} %bitcast.16, f32[48,128]{1,0:T(8,128)} %bitcast.18, ...), custom_call_target="tpu_custom_call" | custom-call | flops 8999999488 | bytes 12000000 | tf_op jit(solution)/shard_map/parallel_block_backward/pallas_call | solution.py:675
  125.6 2.8 %results.1 = (bf16[192,384]{1,0:T(8,128)(2,1)}, f32[1,192]{1,0:T(1,128)}, f32[768,384]{1,0:T(8,128)}, f32[384,768]{1,0:T(8,128)}) custom-call(bf16[192,384]{1,0:T(8,128)(2,1)} %get-tuple-element.12.refs_0_, f32[1,192]{1,0:T(1,128)} %get-tuple-element.13.refs_1_, f32[768,384]{1,0:T(8,128)} %get-tuple-element.14.refs_2_, f32[384,768]{1,0:T(8,128)} %get-tuple-element.15.refs_3_), custom_call_target="tpu_custom_call" | custom-call | tf_op jit(solution)/shard_map/results/pallas_call | solution.py:694

commit v4 on v3

--- a/solution.py
+++ b/solution.py
@@ -34,8 +34,8 @@
 
 def kernel(
     x_in, g_in, attn, gain, w_in, w_out,
-    dx_out, gg_out, dwin_out, dwout_out,
-    XG, XS, XN, WI, WT, WO, HB, GB, PRE, ACT, SL, WG, SM, SV, ST, R1, R2, R3, R4, TS, MO, GP,
+    dx_out, gg_out, dwin_out, dwout_hbm,
+    XG, XS, XN, WI, WT, WO, HB, GB, PRE, ACT, SL, WG, dwout_out, SM, SV, ST, R1, R2, R3, R4, TS, MO, GP,
     zs, zr, as_, ar, z2s, z2r, a2s, a2r, ps, pr, hs, hr, z4s, z4r, xs, xr, xbs, xbr, half_in, line_in, x_in_, y_in_,
     r1s, r1r, r2s, r2r, r3s, r3r, r4s, r4r, sts, str_, mos, mor, gps, gpr, loc,
 ):
@@ -588,8 +588,11 @@
     gg_out[...] = total[0:1, 0:ROWS]
     norm_of(1 - h)
     sum_out(1 - h)
+    leave = pltpu.make_async_copy(dwout_out, dwout_hbm, loc.at[21])
+    leave.start()
     step(hg, 4)
     sum_in(1 - h)
+    leave.wait()
 
     for made in sends:
         made.wait_send()
@@ -651,6 +654,7 @@
         pltpu.VMEM((HID, TOK), F32),
         pltpu.VMEM((HID, TOK), F32),
         pltpu.VMEM((HID, 128), F32),
+        pltpu.VMEM((HID, 768), F32),
         pltpu.VMEM((16, TOK), F32),
         pltpu.VMEM((16, TOK), F32),
         pltpu.VMEM((8, 8, TOK), F32),
@@ -665,7 +669,7 @@
     scratch += pair(2, 4) + pair(8, 8) + pair(4) + pair(4, 8) + [dma((2,)), dma]
     scratch += pair(2, 2, 4) + pair(2) + pair(2, 2, 4) + pair(2, 2, 4)
     scratch += [pltpu.SemaphoreType.REGULAR] * 4
-    scratch += pair(4, 4) + pair(2, 4) + pair(2, 4) + pair(4) + pair(8) + pair(7) + pair(8) + [dma((21,))]
+    scratch += pair(4, 4) + pair(2, 4) + pair(2, 4) + pair(4) + pair(8) + pair(7) + pair(8) + [dma((22,))]
     shapes = (
         jax.ShapeDtypeStruct((ROWS, TOK), BF16),
         jax.ShapeDtypeStruct((1, ROWS), F32),
@@ -676,7 +680,7 @@
         kernel,
         out_shape=shapes,
         in_specs=[anywhere, anywhere, vmem, vmem, anywhere, anywhere],
-        out_specs=(vmem,) * 4,
+        out_specs=(vmem, vmem, vmem, anywhere),
         scratch_shapes=scratch,
         compiler_params=pltpu.CompilerParams(
             collective_id=0, has_side_effects=True, vmem_limit_bytes=62 * 2**20

time: 129 us -> 128 us (level)
  no operation moved by 1% of the time
where the time goes in v4:
time: 128 us
  Pallas kernels  127 us (99%)
    pallas_call x1, Pallas kernels, on_device(): pl.pallas_call(kernel, out_shape=shapes, in_specs=[anywhere, anywhere, vm...  125 us
    pallas_call x1, Pallas kernels, on_device(): pl.pallas_call(hand_over, out_shape=shapes, in_specs=[anywhere] * 4, out_...  2.83 us

profile of v4, /device:TPU:97, one launch (start us, length us, event | category | flops | bytes accessed | tf_op | source)
XLA Modules:
  0.0 128.2 jit_solution(967717740107492352)
XLA Ops:
  0.6 124.5 %parallel_block_backward.1 = (bf16[192,384]{1,0:T(8,128)(2,1)}, f32[1,192]{1,0:T(1,128)}, f32[768,384]{1,0:T(8,128)}, f32[384,768]{1,0:T(8,128)}) custom-call(bf16[2,96,384]{2,1,0:T(8,128)(2,1)} %bitcast.14, bf16[2,96,384]{2,1,0:T(8,128)(2,1)} %bitcast.15, bf16[2,96,384]{2,1,0:T(8,128)(2,1)} %bitcast.16, f32[48,128]{1,0:T(8,128)} %bitcast.18, ...), custom_call_target="tpu_custom_call" | custom-call | flops 8999999488 | bytes 12000000 | tf_op jit(solution)/shard_map/parallel_block_backward/pallas_call | solution.py:679
  125.2 2.8 %results.1 = (bf16[192,384]{1,0:T(8,128)(2,1)}, f32[1,192]{1,0:T(1,128)}, f32[768,384]{1,0:T(8,128)}, f32[384,768]{1,0:T(8,128)}) custom-call(bf16[192,384]{1,0:T(8,128)(2,1)} %get-tuple-element.12.refs_0_, f32[1,192]{1,0:T(1,128)} %get-tuple-element.13.refs_1_, f32[768,384]{1,0:T(8,128)} %get-tuple-element.14.refs_2_, f32[384,768]{1,0:T(8,128)} %get-tuple-element.15.refs_3_), custom_call_target="tpu_custom_call" | custom-call | tf_op jit(solution)/shard_map/results/pallas_call | solution.py:698
